TPU v7x, 256 devices: a whole 4x4x8 slice. The times are simulated.
256 devices in a mesh: chan: 64 (over x, z_hi, y), tile: 4 (over z_lo, core).
Axes of the slice: x: 4, y: 4, z: 8 (z_hi: 4, z_lo: 2; z = z_hi * 2 + z_lo), core: 2. Of those that a mesh axis runs over, the one named last changes fastest.
Arguments:
- cube: float32 [512, 512, 1024], P('chan', 'tile'), may hold values from -6 to 6
- residual_op: float32 [512, 512], replicated, may hold values from -0.25 to 0.25
- taper_x: float32 [512], P('tile'), may hold values from 0.2 to 1
- taper_y: float32 [1024], replicated, may hold values from 0.2 to 1
Outputs:
- spectrum: bfloat16 [2, 512, 512, 1024], P(None, 'chan', None, 'tile')
All inputs are finite; a program needn't handle non-finite values.
Results may differ from a plain program's by a relative error of at most 0.0069.
Values may be sent and summed in bfloat16 or wider, within the bound.
A program may use at most 64 MiB of HBM per device.

v0:
```python
import math

import jax
import jax.numpy as jnp
from jax import lax
from jax.sharding import PartitionSpec as P


def tables(count):
    index = jnp.arange(count, dtype=jnp.int32)
    product = index[:, None] * index[None, :] % count
    angle = 2.0 * math.pi / count * product.astype(jnp.float32)
    scale = 1.0 / math.sqrt(count)
    return (
        (jnp.cos(angle) * scale).astype(jnp.bfloat16),
        (-jnp.sin(angle) * scale).astype(jnp.bfloat16),
    )


def row_transform(image):
    width_y = image.shape[-1]
    cos_y, msin_y = tables(width_y)
    flat = image.reshape(-1, width_y)
    row_re = jnp.dot(flat, cos_y, preferred_element_type=jnp.float32).astype(jnp.bfloat16)
    row_im = jnp.dot(flat, msin_y, preferred_element_type=jnp.float32).astype(jnp.bfloat16)
    return jnp.stack([row_re, row_im]).reshape((2,) + image.shape)


def shards(cube, residual_op, taper_x, taper_y):
    groups = lax.axis_size("chan")
    ch_local, rows_tile, width_y = cube.shape
    rows_pencil = rows_tile // groups
    blocks = cube.reshape(ch_local, groups, rows_pencil * width_y)
    resid = jnp.dot(
        residual_op,
        lax.all_to_all(blocks, "chan", split_axis=1, concat_axis=0, tiled=True)[:, 0, :],
        precision=lax.Precision.HIGHEST,
        preferred_element_type=jnp.float32,
    )
    channels = resid.shape[0]
    resid = resid.reshape(channels, rows_pencil, width_y)
    start = lax.axis_index("chan") * rows_pencil
    local_taper = lax.dynamic_slice_in_dim(taper_x, start, rows_pencil, 0)
    tapered = (resid * local_taper[None, :, None] * taper_y[None, None, :]).astype(jnp.bfloat16)
    rows = row_transform(tapered)
    rows = lax.all_to_all(rows, "chan", split_axis=1, concat_axis=2, tiled=True)
    columns = lax.all_to_all(rows, "tile", split_axis=3, concat_axis=2, tiled=True)
    width_x = columns.shape[2]
    cos_x, msin_x = tables(width_x)
    real_part = columns[0]
    imag_part = columns[1]
    out_re = jnp.einsum(
        "kx,cxy->cky", cos_x, real_part, preferred_element_type=jnp.float32
    ) - jnp.einsum("kx,cxy->cky", msin_x, imag_part, preferred_element_type=jnp.float32)
    out_im = jnp.einsum(
        "kx,cxy->cky", cos_x, imag_part, preferred_element_type=jnp.float32
    ) + jnp.einsum("kx,cxy->cky", msin_x, real_part, preferred_element_type=jnp.float32)
    return jnp.stack([out_re, out_im]).astype(jnp.bfloat16)


def solution(mesh):
    placed = (P("chan", "tile", None), P(), P("tile"), P())
    return jax.shard_map(
        shards, mesh=mesh, in_specs=placed, out_specs=P(None, "chan", None, "tile"), check_vma=False
    )
```

profile of v0, /device:TPU:1, one launch (start us, length us, event | category | flops | bytes accessed | tf_op | source)
XLA Modules:
  0.0 413.1 jit_solution(9470375564277043876)
XLA Ops:
  0.0 5.3 %reshape.20 = f32[8,64,2048]{2,1,0:T(8,128)} reshape(f32[8,128,1024]{2,1,0:T(8,128)} %param.4) | data formatting | bytes 8388608 | tf_op jit(solution)/shard_map/reshape | solution.py:33
  5.3 6.6 %copy.35 = f32[8,64,2048]{2,0,1:T(8,128)} copy(f32[8,64,2048]{2,1,0:T(8,128)} %reshape.20) | data formatting | bytes 8388608 | tf_op jit(solution)/shard_map/reshape | solution.py:33
  11.9 16.0 %all-to-all-start = ((f32[8,64,2048]{2,0,1:T(8,128)}), f32[8,64,2048]{2,0,1:T(8,128)}, u32[]{:S(2)}, u32[]{:S(2)}) async-start(f32[8,64,2048]{2,0,1:T(8,128)} %copy.35), calls=%async_computation | async-start | bytes 8388608 | tf_op jit(solution)/shard_map/all_to_all | solution.py:36
  28.0 94.9 %all-to-all-done = f32[8,64,2048]{2,0,1:T(8,128)} async-done(((f32[8,64,2048]{2,0,1:T(8,128)}), f32[8,64,2048]{2,0,1:T(8,128)}, u32[]{:S(2)}, u32[]{:S(2)}) %all-to-all-start) | async-done | bytes 4194336 | tf_op jit(solution)/shard_map/all_to_all | solution.py:36
  122.9 5.3 %copy.36 = f32[2048,512]{1,0:T(8,128)} copy(f32[2048,512]{0,1:T(8,128)} %bitcast.4) | data formatting | bytes 8388608 | tf_op jit(solution)/shard_map/dot_general | solution.py:34
  128.3 8.8 %multiply_convert_fusion.2 = bf16[512,2,1024]{2,0,1:T(8,128)(2,1)S(1)} fusion(f32[2,1024,512]{2,1,0:T(8,128)} %bitcast.50, f32[1024]{0:T(1024)S(1)} %copy-done.5, f32[2]{0:T(128)S(1)} %dynamic_slice.3, f32[512,512]{1,0:T(8,128)S(1)} %copy-done), kind=kOutput, calls=%fused_computation.15 | convolution fusion | flops 6445596672 | bytes 7344136 | tf_op jit(solution)/shard_map/dot_general | solution.py:34
  139.2 2.2 reshape.21
  141.5 19.1 %fusion.12 = bf16[1024,1024]{1,0:T(8,128)(2,1)S(1)} fusion(bf16[1024,1024]{1,0:T(8,128)(2,1)} %reshape.21), kind=kOutput, calls=%fused_computation.21 | convolution fusion | flops 2166358016 | bytes 4194304 | tf_op jit(solution)/shard_map/dot_general | solution.py:25
  160.6 20.3 %fusion.13 = bf16[1024,1024]{1,0:T(8,128)(2,1)} fusion(bf16[1024,1024]{1,0:T(8,128)(2,1)S(1)} %copy-done.4), kind=kOutput, calls=%fused_computation.22 | convolution fusion | flops 2165309440 | bytes 4194304 | tf_op jit(solution)/shard_map/dot_general | solution.py:24
  181.0 4.1 stack.21
  187.3 7.6 %pad_maximum_fusion = bf16[2,512,2,1024]{3,2,0,1:T(2,128)(2,1)S(1)} fusion(bf16[1,512,2,1024]{3,2,0,1:T(2,128)(2,1)} %bitcast.54, bf16[1,512,2,1024]{3,2,0,1:T(2,128)(2,1)} %bitcast.53), kind=kLoop, calls=%fused_computation.6 | loop fusion | flops 2097152 | bytes 8388608 | tf_op jit(solution)/shard_map/stack | solution.py:26
  194.9 104.7 %all_to_all.48 = bf16[2,512,2,1024]{3,2,0,1:T(2,128)(2,1)S(1)} all-to-all(bf16[2,512,2,1024]{3,2,0,1:T(2,128)(2,1)S(1)} %pad_maximum_fusion), channel_id=1, replica_groups=mesh['chan'=64,'tile'=4] {'chan'}, dimensions={1} | all-to-all | bytes 8388608 | tf_op jit(solution)/shard_map/all_to_all | solution.py:46
  300.9 2.5 copy.41
  303.4 7.3 %copy.42 = bf16[2,8,128,1024]{2,1,0,3:T(8,128)(2,1)} copy(bf16[2,8,128,1024]{3,1,2,0:T(8,128)(2,1)} %bitcast.52) | data formatting | bytes 8388608 | tf_op jit(solution)/shard_map/all_to_all | solution.py:46
  310.6 54.3 %all_to_all.49 = bf16[2,8,128,1024]{2,1,0,3:T(8,128)(2,1)S(1)} all-to-all(bf16[2,8,128,1024]{2,1,0,3:T(8,128)(2,1)} %copy.42), channel_id=1, replica_groups=mesh['chan'=64,'tile'=4] {'tile'}, dimensions={3} | all-to-all | bytes 8388608 | tf_op jit(solution)/shard_map/all_to_all | solution.py:47
  369.3 2.2 squeeze.10
  371.5 3.2 copy.45
  374.8 2.2 squeeze.11
  377.0 6.5 %fusion.27 = f32[8,256,512]{2,1,0:T(8,128)S(1)} fusion(bf16[8,512,256]{1,2,0:T(8,128)(2,1)} %squeeze.11), kind=kOutput, calls=%fused_computation.39 | convolution fusion | flops 1077936128 | bytes 6291456 | tf_op jit(solution)/shard_map/kx,cxy->cky/dot_general | solution.py:55
  383.5 7.5 %fusion.29 = f32[8,256,512]{2,1,0:T(8,128)S(1)} fusion(bf16[8,512,256]{1,2,0:T(8,128)(2,1)S(1)} %copy-done.2), kind=kOutput, calls=%fused_computation.40 | convolution fusion | flops 1077936128 | bytes 6291456 | tf_op jit(solution)/shard_map/kx,cxy->cky/dot_general | solution.py:52
  391.0 6.7 %fusion.15 = bf16[1,8,512,256]{2,3,1,0:T(8,128)(2,1)S(1)} fusion(f32[8,256,512]{2,1,0:T(8,128)S(1)} %fusion.27, bf16[8,512,256]{1,2,0:T(8,128)(2,1)S(1)} %copy-done.2), kind=kOutput, calls=%fused_computation.24 | convolution fusion | flops 1080295424 | bytes 8388608 | tf_op jit(solution)/shard_map/kx,cxy->cky/dot_general | solution.py:57
  397.7 6.7 %fusion.14 = bf16[1,8,512,256]{2,3,1,0:T(8,128)(2,1)S(1)} fusion(f32[8,256,512]{2,1,0:T(8,128)S(1)} %fusion.29, bf16[8,512,256]{1,2,0:T(8,128)(2,1)S(1)} %copy-done.3), kind=kOutput, calls=%fused_computation.23 | convolution fusion | flops 1080295424 | bytes 8388608 | tf_op jit(solution)/shard_map/kx,cxy->cky/dot_general | solution.py:54
  404.4 2.3 pad_maximum_fusion.1
  406.7 6.2 %copy.46 = bf16[2,8,512,256]{3,2,1,0:T(8,128)(2,1)} copy(bf16[2,8,512,256]{2,3,1,0:T(8,128)(2,1)} %pad_maximum_fusion.1) | data formatting | bytes 8388608 | tf_op jit(solution)/shard_map/stack | solution.py:58
  (21 shorter events, 10.2 us)
Async XLA Ops:
  0.0 128.3 %copy-start = (f32[512,512]{1,0:T(8,128)S(1)}, f32[512,512]{1,0:T(8,128)}, u32[]{:S(2)}) copy-start(f32[512,512]{1,0:T(8,128)} %param.5) | copy-start | bytes 3145732
  11.9 16.1 %copy-start.6 = (f32[128]{0:T(128)S(1)}, f32[128]{0:T(128)}, u32[]{:S(2)}) copy-start(f32[128]{0:T(128)} %param.6) | copy-start | bytes 1540
  11.9 111.0 %all-to-all-start = ((f32[8,64,2048]{2,0,1:T(8,128)}), f32[8,64,2048]{2,0,1:T(8,128)}, u32[]{:S(2)}, u32[]{:S(2)}) async-start(f32[8,64,2048]{2,0,1:T(8,128)} %copy.35), calls=%async_computation | async-start | bytes 8388608 | tf_op jit(solution)/shard_map/all_to_all | solution.py:36
  122.9 5.4 %copy-start.5 = (f32[1024]{0:T(1024)S(1)}, f32[1024]{0:T(1024)}, u32[]{:S(2)}) copy-start(f32[1024]{0:T(1024)} %param.7) | copy-start | bytes 12292
  141.5 19.2 %copy-start.4 = (bf16[1024,1024]{1,0:T(8,128)(2,1)S(1)}, bf16[1024,1024]{1,0:T(8,128)(2,1)}, u32[]{:S(2)}) copy-start(bf16[1024,1024]{1,0:T(8,128)(2,1)} %reshape.21) | copy-start | bytes 6291460
  377.0 6.5 %copy-start.2 = (bf16[8,512,256]{1,2,0:T(8,128)(2,1)S(1)}, bf16[8,512,256]{1,2,0:T(8,128)(2,1)}, u32[]{:S(2)}) copy-start(bf16[8,512,256]{1,2,0:T(8,128)(2,1)} %squeeze.10) | copy-start | bytes 6291460
  391.0 6.7 %copy-start.3 = (bf16[8,512,256]{1,2,0:T(8,128)(2,1)S(1)}, bf16[8,512,256]{1,2,0:T(8,128)(2,1)}, u32[]{:S(2)}) copy-start(bf16[8,512,256]{1,2,0:T(8,128)(2,1)} %squeeze.11) | copy-start | bytes 6291460
  404.4 8.5 %copy-start.1 = (f32[512,512]{1,0:T(8,128)S(1)}, f32[512,512]{1,0:T(8,128)}, u32[]{:S(2)}) copy-start(f32[512,512]{1,0:T(8,128)} %param.5) | copy-start | bytes 3145732
where the time goes:
time: 417 us; the launch traced here: 413 us
  blocking collectives  159 us (38%)
  waiting for transfers between devices  94.9 us (23%)
  matrix products  75.6 us (18%)
  local copies, waits for them, and re-layouts  57.4 us (14%)
  starting transfers between devices  16 us (4%)
  other arithmetic  9.93 us (2%)
    all_to_all x1, blocking collectives, shards(): rows = lax.all_to_all(rows, 'chan', split_axis=1, concat_axis=2, tiled=True)  105 us
    all_to_all x1, waiting for transfers between devices, shards(): lax.all_to_all(blocks, 'chan', split_axis=1, concat_axis=0, tiled=True)  94.9 us
    all_to_all x1, blocking collectives, shards(): lax.all_to_all(rows, 'tile', split_axis=3, concat_axis=2, tiled=True)  54.3 us
    dot_general x1, matrix products, row_transform(): jnp.dot(flat, cos_y, preferred_element_type=jnp.float32)  20.3 us
    dot_general x1, matrix products, row_transform(): jnp.dot(flat, msin_y, preferred_element_type=jnp.float32)  19.1 us
    all_to_all x1, starting transfers between devices, shards(): lax.all_to_all(blocks, 'chan', split_axis=1, concat_axis=0, tiled=True)  16 us
    reshape x2, local copies, waits for them, and re-layouts, shards(): blocks = cube.reshape(ch_local, groups, rows_pencil * width_y)  11.9 us
    all_to_all x3, local copies, waits for them, and re-layouts, shards(): rows = lax.all_to_all(rows, 'chan', split_axis=1, concat_axis=2, tiled=True)  11.1 us
  transfers between devices with their start and end apart: 1, of which 1 were waited for; matrix products, arithmetic and copies ran while one was open for 0% of the time, Pallas kernels for 0%

commit v1 on v0

v1 whole, which is shorter than its diff:
```python
import functools
import math

import jax
import jax.numpy as jnp
import ml_dtypes
import numpy as np
from jax import lax
from jax.experimental import pallas as pl
from jax.experimental.pallas import tpu as pltpu
from jax.sharding import PartitionSpec as P

MESH = pl.DeviceIdType.MESH
BF16 = jnp.bfloat16
F32 = jnp.float32
NX, NY = 512, 1024
PEERS = 63 + 32 + 2


def tables(count):
    index = np.arange(count, dtype=np.int64)
    angle = 2.0 * math.pi / count * ((index[:, None] * index[None, :]) % count)
    scale = 1.0 / math.sqrt(count)
    return (np.cos(angle) * scale).astype(np.float32), (-np.sin(angle) * scale).astype(np.float32)


def row_tables():
    cos_y, msin_y = tables(NY)
    parts = [np.concatenate([cos_y[:, 256 * t:256 * t + 256], msin_y[:, 256 * t:256 * t + 256]], 1) for t in range(4)]
    return np.stack(parts).astype(ml_dtypes.bfloat16)


def column_table():
    cos_x, msin_x = tables(NX)
    tile, zh, r, cx, cy = np.meshgrid(*[np.arange(n) for n in (4, 4, 2, 4, 4)], indexing="ij")
    order = (tile * 128 + r * 64 + cx * 16 + zh * 4 + cy).reshape(-1)
    cos_x, msin_x = cos_x[:, order], msin_x[:, order]
    whole = np.concatenate([np.concatenate([cos_x, -msin_x], 1), np.concatenate([msin_x, cos_x], 1)], 0)
    return whole.astype(ml_dtypes.bfloat16)


def mix_rows(cube, op, taper_x, taper_y, ytab, rows_out,
             held, sent, mixed_in, op2, tapered, land, table, wide, rows,
             cube_sem, table_sem, out_sem, send1, recv1, send2, land_sem,
             send_fwd, fwd_sem, send_sib, sib_sem, sibf_sem):
    c = lax.axis_index("chan")
    t = lax.axis_index("tile")
    x, j, y = c // 16, (c // 4) % 4, c % 4
    zl, co = t // 2, t % 2
    u = 1 - 2 * zl
    partner = (c, (1 - zl) * 2 + co)
    sibling = (c, zl * 2 + 1 - co)

    loads = [pltpu.make_async_copy(cube.at[:, pl.ds(128 * k, 128)], held.at[k], cube_sem.at[k]) for k in range(8)]
    for load in loads:
        load.start()
    table_load = pltpu.make_async_copy(ytab.at[t], table, table_sem)
    table_load.start()

    barrier = pltpu.get_barrier_semaphore()

    def greet(k, _):
        pl.semaphore_signal(barrier, inc=1, device_id=((c + k) % 64, t), device_id_type=MESH)
        return 0

    lax.fori_loop(1, 64, greet, 0)

    def greet_far(k, _):
        near = (j - u + 4) % 4
        far = (j + 2) % 4
        base = (k // 4) * 16 + k % 4
        for zh in (near, far):
            pl.semaphore_signal(barrier, inc=1, device_id=(base + zh * 4, (1 - zl) * 2 + co), device_id_type=MESH)
        return 0

    lax.fori_loop(0, 16, greet_far, 0)
    for other in (partner, sibling):
        pl.semaphore_signal(barrier, inc=1, device_id=other, device_id_type=MESH)

    for k in range(8):
        loads[k].wait()

        def cast(o, _, k=k):
            block = held[k, pl.ds(o, 16, stride=64), :]
            sent[pl.ds(pl.multiple_of(o * 16, 16), 16), 128 * k:128 * k + 128] = block.astype(BF16)
            return 0

        lax.fori_loop(0, 64, cast, 0, unroll=8)

    pl.semaphore_wait(barrier, PEERS)

    mine = pl.ds(pl.multiple_of(c * 16, 16), 16)
    own1 = pltpu.make_async_copy(sent.at[mine], mixed_in.at[mine], recv1)
    own1.start()

    def scatter(k, _):
        d = (c + k) % 64
        pltpu.make_async_remote_copy(
            src_ref=sent.at[pl.ds(pl.multiple_of(d * 16, 16), 16)], dst_ref=mixed_in.at[mine],
            send_sem=send1, recv_sem=recv1, device_id=(d, t), device_id_type=MESH).start()
        return 0

    lax.fori_loop(1, 64, scatter, 0)

    c2 = lax.broadcasted_iota(jnp.int32, (512, 1024), 0)
    spread_k = jnp.where(lax.broadcasted_iota(jnp.int32, (512, 1024), 1) // 2 == c2, 1.0, 0.0).astype(BF16)
    i = lax.broadcasted_iota(jnp.int32, (256, 512), 0)
    cc = lax.broadcasted_iota(jnp.int32, (256, 512), 1)
    same = (lax.broadcasted_iota(jnp.int32, (256, 1024), 0) % 2) == (lax.broadcasted_iota(jnp.int32, (256, 1024), 1) % 2)
    op_low = op[...].astype(BF16)

    def expand(zh, _):
        pick = jnp.where((i // 64) * 128 + zh * 32 + (i % 64) // 2 == cc, 1.0, 0.0).astype(BF16)
        some = jnp.dot(pick, op_low, preferred_element_type=F32).astype(BF16)
        full = jnp.dot(some, spread_k, preferred_element_type=F32)
        op2[pl.ds(pl.multiple_of(zh * 256, 256), 256), :] = jnp.where(same, full, 0.0).astype(BF16)
        return 0

    lax.fori_loop(0, 4, expand, 0)
    odd = lax.broadcasted_iota(jnp.int32, (256, 256), 0) % 2 == 1
    tx = jnp.where(odd, taper_x[0, c + 64], taper_x[0, c])
    table_load.wait()

    pltpu.make_async_copy(sent, mixed_in, recv1).wait()

    def mix(st, _):
        delta = jnp.where(st == 0, 0, jnp.where(st == 1, -u, jnp.where(st == 2, u, 2)))
        zh = (j + delta + 4) % 4
        start = pl.multiple_of(zh * 256, 256)

        def strip(n, _):
            cols = pl.ds(pl.multiple_of(n * 256, 256), 256)
            part = jnp.dot(op2[pl.ds(start, 256), :], mixed_in[:, cols], preferred_element_type=F32)
            tapered[pl.ds(start, 256), cols] = (part * tx * taper_y[:, cols]).astype(BF16)
            return 0

        lax.fori_loop(0, 4, strip, 0)
        far = st % 2
        to_tile = jnp.where(far == 1, (1 - zl) * 2 + co, t)

        def scatter2(k, _):
            dx = (x + k // 4) % 4
            dy = (y + k % 4) % 4
            src = tapered.at[pl.ds(pl.multiple_of(start + dx * 64 + dy * 16, 16), 16)]
            dst = land.at[t * 4 + j, pl.ds(pl.multiple_of(x * 64 + y * 16, 16), 16)]
            pltpu.make_async_remote_copy(
                src_ref=src, dst_ref=dst, send_sem=send2, recv_sem=land_sem.at[st * 4 + k // 4],
                device_id=(dx * 16 + zh * 4 + dy, to_tile), device_id_type=MESH).start()
            return 0

        first = jnp.where(st == 0, 1, 0)
        lax.fori_loop(first, 16, scatter2, 0)
        return 0

    lax.fori_loop(0, 4, mix, 0)
    own2 = pltpu.make_async_copy(
        tapered.at[pl.ds(pl.multiple_of(j * 256 + x * 64 + y * 16, 16), 16)],
        land.at[t * 4 + j, pl.ds(pl.multiple_of(x * 64 + y * 16, 16), 16)], land_sem.at[0])
    own2.start()

    def group_of(st, passed, other_core):
        z = zl + passed - 2 * zl * passed
        v = 1 - 2 * z
        h = (z + st) % 2
        zh = (j - jnp.where(st == 0, 0, jnp.where(st == 3, 2, v)) + 4) % 4
        core = co + other_core - 2 * co * other_core
        return (h * 2 + core) * 4 + zh

    def piece(st, e, passed, other_core):
        xs = (x - e + 4) % 4
        return land.at[group_of(st, passed, other_core), pl.ds(pl.multiple_of(xs * 64, 64), 64)]

    def arrived(ref, sem):
        pltpu.make_async_copy(ref, ref, sem).wait()

    def pass_on(ref, send, recv, device):
        pltpu.make_async_remote_copy(src_ref=ref, dst_ref=ref, send_sem=send, recv_sem=recv,
                                     device_id=device, device_id_type=MESH).start()

    def take_landed(n):
        st, e = n // 4, n % 4
        ref = piece(st, e, 0, 0)
        arrived(ref, land_sem.at[n])
        pass_on(ref, send_fwd, fwd_sem.at[n], partner)
        pass_on(ref, send_sib, sib_sem.at[n], sibling)

    def take_passed(n):
        st, e = n // 4, n % 4
        ref = piece(st, e, 1, 0)
        arrived(ref, fwd_sem.at[n])
        pass_on(ref, send_sib, sibf_sem.at[n], sibling)

    def take_sibling(st, passed, sem):
        for e in range(4):
            arrived(piece(st, e, passed, 1), sem.at[st * 4 + e])

    def transform(g):
        for n in range(2):
            part = jnp.dot(land[g], table[:, 256 * n:256 * n + 256], preferred_element_type=F32)
            wide[2 * n] = part[:, :128]
            wide[2 * n + 1] = part[:, 128:]
        for q in range(16):
            ch, r = q // 2, q % 2
            for n in range(4):
                at = pl.ds(pl.multiple_of(g * 32 + r * 16, 16), 16)
                rows[ch, n // 2, at, (n % 2) * 128:(n % 2) * 128 + 128] = wide[n, pl.ds(q, 16, stride=16), :].astype(BF16)
        span = pl.ds(pl.multiple_of(g * 32, 32), 32)
        pltpu.make_async_copy(rows.at[:, :, span], rows_out.at[:, :, span], out_sem).start()

    def first_pieces(n, _):
        take_landed(n)
        return 0

    lax.fori_loop(0, 4, first_pieces, 0)
    take_passed(0)
    take_passed(1)

    def stage(st, _):
        last = st - 1
        take_landed(st * 4)
        take_passed(st * 4 - 2)
        transform(group_of(last, 0, 0))
        take_landed(st * 4 + 1)
        take_passed(st * 4 - 1)
        take_sibling(last, 0, sib_sem)
        transform(group_of(last, 0, 1))
        take_landed(st * 4 + 2)
        take_passed(st * 4)
        transform(group_of(last, 1, 0))
        take_landed(st * 4 + 3)
        take_passed(st * 4 + 1)
        take_sibling(last, 1, sibf_sem)
        transform(group_of(last, 1, 1))
        return 0

    lax.fori_loop(1, 4, stage, 0)
    transform(group_of(3, 0, 0))
    take_passed(14)
    take_sibling(3, 0, sib_sem)
    transform(group_of(3, 0, 1))
    take_passed(15)
    transform(group_of(3, 1, 0))
    take_sibling(3, 1, sibf_sem)
    transform(group_of(3, 1, 1))

    pltpu.make_async_copy(rows, rows_out, out_sem).wait()
    less = pl.ds(0, 63 * 16)
    pltpu.make_async_copy(sent.at[less], mixed_in.at[less], send1).wait()
    pltpu.make_async_copy(tapered.at[less], tapered.at[less], send2).wait()
    pltpu.make_async_copy(land.at[pl.ds(0, 4)], land.at[pl.ds(0, 4)], send_fwd).wait()
    pltpu.make_async_copy(land.at[pl.ds(0, 8)], land.at[pl.ds(0, 8)], send_sib).wait()


def columns(table, rows, out):
    both = jnp.dot(table[...], rows[0], preferred_element_type=F32).astype(BF16)
    out[0, 0] = both[:512]
    out[1, 0] = both[512:]


def shards(cube, residual_op, taper_x, taper_y):
    vmem = pl.BlockSpec(memory_space=pltpu.VMEM)
    hbm = pl.BlockSpec(memory_space=pl.ANY)
    dma = pltpu.SemaphoreType.DMA
    rows = pl.pallas_call(
        mix_rows,
        name="mix_rows",
        out_shape=jax.ShapeDtypeStruct((8, 2, 512, 256), BF16),
        in_specs=[hbm, vmem, pl.BlockSpec(memory_space=pltpu.SMEM), vmem, hbm],
        out_specs=hbm,
        scratch_shapes=[
            pltpu.VMEM((8, 1024, 128), F32),
            pltpu.VMEM((1024, 1024), BF16),
            pltpu.VMEM((1024, 1024), BF16),
            pltpu.VMEM((1024, 1024), BF16),
            pltpu.VMEM((1024, 1024), BF16),
            pltpu.VMEM((16, 256, 1024), BF16),
            pltpu.VMEM((1024, 512), BF16),
            pltpu.VMEM((4, 256, 128), F32),
            pltpu.VMEM((8, 2, 512, 256), BF16),
            dma((8,)), dma, dma, dma, dma, dma, dma((16,)),
            dma, dma((16,)), dma, dma((16,)), dma((16,)),
        ],
        compiler_params=pltpu.CompilerParams(
            collective_id=0, has_side_effects=True, vmem_limit_bytes=56 << 20),
        cost_estimate=pl.CostEstimate(flops=8 << 30, bytes_accessed=16 << 20, transcendentals=0),
    )(cube.reshape(1024, 1024), residual_op, taper_x.reshape(1, 128), taper_y.reshape(1, 1024), jnp.asarray(row_tables()))
    return pl.pallas_call(
        columns,
        name="columns",
        grid=(8,),
        out_shape=jax.ShapeDtypeStruct((2, 8, 512, 256), BF16),
        in_specs=[pl.BlockSpec((1024, 1024), lambda ch: (0, 0)), pl.BlockSpec((1, 1024, 256), lambda ch: (ch, 0, 0))],
        out_specs=pl.BlockSpec((2, 1, 512, 256), lambda ch: (0, ch, 0, 0)),
        compiler_params=pltpu.CompilerParams(vmem_limit_bytes=32 << 20),
        cost_estimate=pl.CostEstimate(flops=4 << 30, bytes_accessed=10 << 20, transcendentals=0),
    )(jnp.asarray(column_table()), rows.reshape(8, 1024, 256))


def solution(mesh):
    placed = (P("chan", "tile", None), P(), P("tile"), P())
    return jax.shard_map(
        shards, mesh=mesh, in_specs=placed, out_specs=P(None, "chan", None, "tile"), check_vma=False
    )
```

time: 417 us -> 149 us (0.36)
  the two profiles are of different devices: /device:TPU:1 before, /device:TPU:47 now
where the time goes in v1:
time: 149 us
  Pallas kernels  147 us (99%)
  local copies, waits for them, and re-layouts  2.18 us (1%)
    pallas_call x1, Pallas kernels, shards(): pl.pallas_call(mix_rows, name='mix_rows', out_shape=jax.ShapeDtypeStruct(...  140 us
    pallas_call x1, Pallas kernels, shards(): pl.pallas_call(columns, name='columns', grid=(8,), out_shape=jax.ShapeDty...  6.74 us

profile of v1, /device:TPU:47, one launch (start us, length us, event | category | flops | bytes accessed | tf_op | source)
XLA Modules:
  0.0 149.4 jit_solution(3632975442802508822)
XLA Ops:
  0.0 0.0 copy-start.1
  0.0 140.4 %mix_rows.1 = bf16[8,2,512,256]{3,2,1,0:T(8,128)(2,1)} custom-call(f32[1024,1024]{1,0:T(8,128)} %bitcast.5, f32[512,512]{1,0:T(8,128)} %op.1, f32[1,128]{1,0:T(1,128)} %bitcast.7, f32[1,1024]{1,0:T(1,128)} %bitcast.6, bf16[4,1024,512]{2,1,0:T(8,128)(2,1)} %constant.4.clone.ytab), custom_call_target="tpu_custom_call" | custom-call | flops 8589934592 | bytes 16777216 | tf_op jit(solution)/shard_map/mix_rows/pallas_call | solution.py:264
  140.4 0.0 copy-done.1
  140.4 0.0 copy-start
  140.4 2.2 %copy-done = bf16[8,2,512,256]{3,2,1,0:T(8,128)(2,1)S(1)} copy-done((bf16[8,2,512,256]{3,2,1,0:T(8,128)(2,1)S(1)}, bf16[8,2,512,256]{3,2,1,0:T(8,128)(2,1)}, u32[]{:S(2)}) %copy-start) | copy-done | bytes 4194328
  142.6 6.7 %columns.1 = bf16[2,8,512,256]{3,2,1,0:T(8,128)(2,1)} custom-call(bf16[1024,1024]{1,0:T(8,128)(2,1)S(1)} %copy-done.1, bf16[8,1024,256]{2,1,0:T(8,128)(2,1)S(1)} %bitcast.4), custom_call_target="tpu_custom_call" | custom-call | flops 4294967296 | bytes 10485760 | tf_op jit(solution)/shard_map/columns/pallas_call | solution.py:287
Async XLA Ops:
  0.0 140.4 %copy-start.1 = (bf16[1024,1024]{1,0:T(8,128)(2,1)S(1)}, bf16[1024,1024]{1,0:T(8,128)(2,1)}, u32[]{:S(2)}) copy-start(bf16[1024,1024]{1,0:T(8,128)(2,1)} %constant.5.clone.table) | copy-start | bytes 6291460
  140.4 2.2 %copy-start = (bf16[8,2,512,256]{3,2,1,0:T(8,128)(2,1)S(1)}, bf16[8,2,512,256]{3,2,1,0:T(8,128)(2,1)}, u32[]{:S(2)}) copy-start(bf16[8,2,512,256]{3,2,1,0:T(8,128)(2,1)} %mix_rows.1) | copy-start | bytes 12582916

commit v2 on v1

v2 whole, which is shorter than its diff:
```python
import functools
import math

import jax
import jax.numpy as jnp
import ml_dtypes
import numpy as np
from jax import lax
from jax.experimental import pallas as pl
from jax.experimental.pallas import tpu as pltpu
from jax.sharding import PartitionSpec as P

MESH = pl.DeviceIdType.MESH
BF16 = jnp.bfloat16
F32 = jnp.float32
NX, NY = 512, 1024
PEERS = 63 + 32 + 2
LAG = 5
EARLY = 8
GROUP = 4


def tables(count):
    index = np.arange(count, dtype=np.int64)
    angle = 2.0 * math.pi / count * ((index[:, None] * index[None, :]) % count)
    scale = 1.0 / math.sqrt(count)
    return (np.cos(angle) * scale).astype(np.float32), (-np.sin(angle) * scale).astype(np.float32)


def row_tables():
    cos_y, msin_y = tables(NY)
    parts = [np.concatenate([cos_y[:, 256 * t:256 * t + 256], msin_y[:, 256 * t:256 * t + 256]], 1) for t in range(4)]
    return np.stack(parts).astype(ml_dtypes.bfloat16)


def column_table():
    cos_x, msin_x = tables(NX)
    par, tile, zh, r, cx, cy = np.meshgrid(*[np.arange(n) for n in (2, 4, 4, 2, 4, 2)], indexing="ij")
    order = (tile * 128 + r * 64 + cx * 16 + zh * 4 + 2 * cy + par).reshape(2, 256)
    halves = []
    for some in order:
        cos_s, msin_s = cos_x[:256, some], msin_x[:256, some]
        halves.append(np.concatenate([np.concatenate([cos_s, -msin_s], 1), np.concatenate([msin_s, cos_s], 1)], 0))
    return np.stack(halves).astype(ml_dtypes.bfloat16)


def mix_rows(cube, op, taper_x, taper_y, ytab, rows_out,
             op_here, held, sent, mixed_in, op2, tapered, land, table, wide, rows,
             cube_sem, table_sem, op_sem, out_sem, send1, recv1, send2, land_sem,
             send_fwd, fwd_sem, send_sib, sib_sem, sibf_sem):
    c = lax.axis_index("chan")
    t = lax.axis_index("tile")
    x, j, y = c // 16, (c // 4) % 4, c % 4
    zl, co = t // 2, t % 2
    u = 1 - 2 * zl
    partner = (c, (1 - zl) * 2 + co)
    sibling = (c, zl * 2 + 1 - co)

    loads = [pltpu.make_async_copy(cube.at[:, pl.ds(128 * k, 128)], held.at[k], cube_sem.at[k]) for k in range(8)]
    for load in loads:
        load.start()
    barrier = pltpu.get_barrier_semaphore()

    def greet(d, _):
        pl.semaphore_signal(barrier, inc=1, device_id=(d, t), device_id_type=MESH)
        return 0

    lax.fori_loop(0, c, greet, 0)
    lax.fori_loop(c + 1, 64, greet, 0)
    near, far = (j - u + 4) % 4, (j + 2) % 4
    across = (1 - zl) * 2 + co
    for cx in range(4):
        def greet_far(cy, _, cx=cx):
            for zh in (near, far):
                pl.semaphore_signal(barrier, inc=1, device_id=(cx * 16 + zh * 4 + cy, across), device_id_type=MESH)
            return 0

        lax.fori_loop(0, 4, greet_far, 0)
    for other in (partner, sibling):
        pl.semaphore_signal(barrier, inc=1, device_id=other, device_id_type=MESH)

    halves = (slice(0, 512), slice(512, 1024))
    mine = pl.ds(pl.multiple_of(c * 16, 16), 16)

    def cast(d, half):
        rows_d = pl.ds(pl.multiple_of(d * 16, 16), 16)
        for k in range(4 * half, 4 * half + 4):
            sent[rows_d, 128 * k:128 * k + 128] = held[k, pl.ds(d, 16, stride=64), :].astype(BF16)
        return sent.at[rows_d, halves[half]]

    for half in range(2):
        for load in loads[4 * half:4 * half + 4]:
            load.wait()
        if half == 0:
            pl.semaphore_wait(barrier, PEERS)
        to = mixed_in.at[mine, halves[half]]

        def scatter(k, _, half=half, to=to):
            d = (c + 21 * k) % 64
            pltpu.make_async_remote_copy(
                src_ref=cast(d, half), dst_ref=to, send_sem=send1, recv_sem=recv1.at[half],
                device_id=(d, t), device_id_type=MESH).start()
            return 0

        lax.fori_loop(1, 64, scatter, 0)
        own1 = pltpu.make_async_copy(cast(c, half), to, recv1.at[half])
        own1.start()

    table_load = pltpu.make_async_copy(ytab.at[t], table, table_sem)
    table_load.start()
    op_load = pltpu.make_async_copy(op, op_here, op_sem)
    op_load.start()

    c2 = lax.broadcasted_iota(jnp.int32, (512, 1024), 0)
    spread_k = jnp.where(lax.broadcasted_iota(jnp.int32, (512, 1024), 1) // 2 == c2, 1.0, 0.0).astype(BF16)
    i = lax.broadcasted_iota(jnp.int32, (256, 512), 0)
    cc = lax.broadcasted_iota(jnp.int32, (256, 512), 1)
    same = (lax.broadcasted_iota(jnp.int32, (256, 1024), 0) % 2) == (lax.broadcasted_iota(jnp.int32, (256, 1024), 1) % 2)
    op_load.wait()
    op_low = op_here[...].astype(BF16)

    def expand(zh, _):
        pick = jnp.where((i // 64) * 128 + zh * 32 + (i % 64) // 2 == cc, 1.0, 0.0).astype(BF16)
        some = jnp.dot(pick, op_low, preferred_element_type=F32).astype(BF16)
        full = jnp.dot(some, spread_k, preferred_element_type=F32)
        op2[pl.ds(pl.multiple_of(zh * 256, 256), 256), :] = jnp.where(same, full, 0.0).astype(BF16)
        return 0

    lax.fori_loop(0, 4, expand, 0)
    odd = lax.broadcasted_iota(jnp.int32, (256, 256), 0) % 2 == 1
    tx = jnp.where(odd, taper_x[0, c + 64], taper_x[0, c])
    table_load.wait()

    def mix(st, half):
        delta = jnp.where(st == 0, 0, jnp.where(st == 1, -u, jnp.where(st == 2, u, 2)))
        zh = (j + delta + 4) % 4
        start = pl.multiple_of(zh * 256, 256)
        for n in range(2):
            cols = slice(512 * half + 256 * n, 512 * half + 256 * n + 256)
            part = jnp.dot(op2[pl.ds(start, 256), :], mixed_in[:, cols], preferred_element_type=F32)
            tapered[pl.ds(start, 256), cols] = (part * tx * taper_y[:, cols]).astype(BF16)
        return zh, start

    here = pl.ds(pl.multiple_of(x * 64 + y * 16, 16), 16)

    def send_rows(st, half, k, zh, start):
        to_tile = jnp.where(st % 2 == 1, across, t)
        dx = (x + k // 4) % 4
        dy = (y + k % 4) % 4
        pltpu.make_async_remote_copy(
            src_ref=tapered.at[pl.ds(pl.multiple_of(start + dx * 64 + dy * 16, 16), 16), halves[half]],
            dst_ref=land.at[t * 4 + j, here, halves[half]], send_sem=send2,
            recv_sem=land_sem.at[half * 16 + st * 4 + k // 4],
            device_id=(dx * 16 + zh * 4 + dy, to_tile), device_id_type=MESH).start()

    def mix_half(half):
        pltpu.make_async_copy(sent.at[:, halves[half]], mixed_in.at[:, halves[half]], recv1.at[half]).wait()
        zh2, start2 = mix(2, half)
        zh0, start0 = mix(0, half)
        send_rows(2, half, 0, zh2, start2)
        own2 = pltpu.make_async_copy(
            tapered.at[pl.ds(pl.multiple_of(start0 + x * 64 + y * 16, 16), 16), halves[half]],
            land.at[t * 4 + j, here, halves[half]], land_sem.at[half * 16])
        own2.start()

        def both(k, _):
            send_rows(2, half, k, zh2, start2)
            send_rows(0, half, k, zh0, start0)
            return 0

        lax.fori_loop(1, 16, both, 0)

        def alone(n, _):
            st = 2 * n + 1
            zh, start = mix(st, half)

            def one(k, _):
                send_rows(st, half, k, zh, start)
                return 0

            lax.fori_loop(0, 16, one, 0)
            return 0

        lax.fori_loop(0, 2, alone, 0)

    def group_of(st, passed, other_core):
        z = zl + passed - 2 * zl * passed
        v = 1 - 2 * z
        h = (z + st) % 2
        zh = (j - jnp.where(st == 0, 0, jnp.where(st == 3, 2, v)) + 4) % 4
        core = co + other_core - 2 * co * other_core
        return (h * 2 + core) * 4 + zh

    def piece(st, e, passed, other_core, half=None):
        xs = (x - e + 4) % 4
        cols = slice(None) if half is None else halves[half]
        return land.at[group_of(st, passed, other_core), pl.ds(pl.multiple_of(xs * 64, 64), 64), cols]

    def arrived(ref, sem):
        pltpu.make_async_copy(ref, ref, sem).wait()

    def pass_on(ref, send, recv, device):
        pltpu.make_async_remote_copy(src_ref=ref, dst_ref=ref, send_sem=send, recv_sem=recv,
                                     device_id=device, device_id_type=MESH).start()

    def place(m):
        st = jnp.where(m < 8, 2 * (m % 2), jnp.where(m < 12, 1, 3))
        return st, jnp.where(m < 8, m // 2, m % 4)

    def take_landed(half, m):
        st, e = place(m)
        ref = piece(st, e, 0, 0, half)
        n = st * 4 + e
        arrived(ref, land_sem.at[half * 16 + n])
        pass_on(ref, send_fwd, fwd_sem.at[half * 16 + n], partner)
        pass_on(ref, send_sib, sib_sem.at[n], sibling)

    def take_passed(half, m):
        st, e = place(m)
        ref = piece(st, e, 1, 0, half)
        n = st * 4 + e
        arrived(ref, fwd_sem.at[half * 16 + n])
        pass_on(ref, send_sib, sibf_sem.at[n], sibling)

    def take_sibling(st, passed, sem):
        for e in range(4):
            arrived(piece(st, e, passed, 1), sem.at[st * 4 + e])

    def transform(g):
        for n in range(2):
            part = jnp.dot(land[g], table[:, 256 * n:256 * n + 256], preferred_element_type=F32)
            wide[2 * n] = part[:, :128]
            wide[2 * n + 1] = part[:, 128:]
        span = pl.ds(pl.multiple_of(g * 16, 16), 16)
        for ch in range(8):
            for par in range(2):
                for n in range(4):
                    two = [wide[n, pl.ds(2 * ch + r + 16 * par, 8, stride=32), :] for r in range(2)]
                    at = 256 * ch + 128 * (n % 2)
                    rows[par, n // 2, span, at:at + 128] = jnp.concatenate(two).astype(BF16)
        pltpu.make_async_copy(rows.at[:, :, span], rows_out.at[:, :, span], out_sem).start()

    mix_half(0)

    def landed0(m, _):
        take_landed(0, m)
        return 0

    def step0(m, _):
        take_landed(0, m)
        take_passed(0, m - LAG)
        return 0

    def step1(m, _):
        take_landed(1, m)
        take_passed(1, m - LAG)
        return 0

    lax.fori_loop(0, LAG, landed0, 0)
    lax.fori_loop(LAG, EARLY, step0, 0)
    mix_half(1)
    lax.fori_loop(max(LAG, EARLY), 16, step0, 0)

    def late(m, _):
        take_landed(1, m)
        take_passed(0, 16 - LAG + m)
        return 0

    lax.fori_loop(0, LAG, late, 0)
    lax.fori_loop(LAG, 8, step1, 0)

    waiting = []
    for m in range(8, 16 + LAG):
        if m < 16:
            take_landed(1, m)
        take_passed(1, m - LAG)
        for done, passed in ((m, 0), (m - LAG, 1)):
            for st, at in ((0, 8), (2, 8), (1, 11), (3, 15)):
                if done == at:
                    waiting += [(st, passed, 0), (st, passed, 1)]
        last = m == 15 + LAG
        for _ in range(len(waiting) if last else min(2, len(waiting))):
            st, passed, other_core = waiting.pop(0)
            if other_core:
                take_sibling(st, passed, sibf_sem if passed else sib_sem)
            transform(group_of(st, passed, other_core))

    pltpu.make_async_copy(rows, rows_out, out_sem).wait()
    less = pl.ds(0, 63 * 16)
    pltpu.make_async_copy(sent.at[less], mixed_in.at[less], send1).wait()
    pltpu.make_async_copy(tapered.at[less], tapered.at[less], send2).wait()
    pltpu.make_async_copy(land.at[pl.ds(0, 4)], land.at[pl.ds(0, 4)], send_fwd).wait()
    pltpu.make_async_copy(land.at[pl.ds(0, 8)], land.at[pl.ds(0, 8)], send_sib).wait()


def columns(table, rows, out, table_here, rows_here, out_here, table_sem, rows_sem, out_sem):
    width = 256 * GROUP
    cols = [slice(width * q, width * q + width) for q in range(8 // GROUP)]
    loads = [pltpu.make_async_copy(table, table_here, table_sem)]
    loads += [pltpu.make_async_copy(rows.at[:, :, some], rows_here.at[:, :, some], rows_sem.at[q]) for q, some in enumerate(cols)]
    for load in loads:
        load.start()
    loads[0].wait()
    stores = []
    for q, some in enumerate(cols):
        loads[1 + q].wait()
        chans = slice(GROUP * q, GROUP * q + GROUP)
        for part in range(2):
            span = slice(256 * part, 256 * part + 256)
            even = jnp.dot(table_here[0, span], rows_here[0, :, some], preferred_element_type=F32)
            odd = jnp.dot(table_here[1, span], rows_here[1, :, some], preferred_element_type=F32)
            plus, minus = (even + odd).astype(BF16), (even - odd).astype(BF16)
            for n in range(GROUP):
                out_here[part, GROUP * q + n, :256] = plus[:, 256 * n:256 * n + 256]
                out_here[part, GROUP * q + n, 256:] = minus[:, 256 * n:256 * n + 256]
            store = pltpu.make_async_copy(out_here.at[part, chans], out.at[part, chans], out_sem.at[part, q])
            store.start()
            stores.append(store)
    for store in stores:
        store.wait()


def shards(cube, residual_op, taper_x, taper_y):
    vmem = pl.BlockSpec(memory_space=pltpu.VMEM)
    hbm = pl.BlockSpec(memory_space=pl.ANY)
    dma = pltpu.SemaphoreType.DMA
    rows = pl.pallas_call(
        mix_rows,
        name="mix_rows",
        out_shape=jax.ShapeDtypeStruct((2, 2, 256, 2048), BF16),
        in_specs=[hbm, hbm, pl.BlockSpec(memory_space=pltpu.SMEM), vmem, hbm],
        out_specs=hbm,
        scratch_shapes=[
            pltpu.VMEM((512, 512), F32),
            pltpu.VMEM((8, 1024, 128), F32),
            pltpu.VMEM((1024, 1024), BF16),
            pltpu.VMEM((1024, 1024), BF16),
            pltpu.VMEM((1024, 1024), BF16),
            pltpu.VMEM((1024, 1024), BF16),
            pltpu.VMEM((16, 256, 1024), BF16),
            pltpu.VMEM((1024, 512), BF16),
            pltpu.VMEM((4, 256, 128), F32),
            pltpu.VMEM((2, 2, 256, 2048), BF16),
            dma((8,)), dma, dma, dma, dma, dma((2,)), dma, dma((32,)),
            dma, dma((32,)), dma, dma((16,)), dma((16,)),
        ],
        compiler_params=pltpu.CompilerParams(
            collective_id=0, has_side_effects=True, vmem_limit_bytes=56 << 20),
        cost_estimate=pl.CostEstimate(flops=8 << 30, bytes_accessed=16 << 20, transcendentals=0),
    )(cube.reshape(1024, 1024), residual_op, taper_x.reshape(1, 128), taper_y.reshape(1, 1024), jnp.asarray(row_tables()))
    return pl.pallas_call(
        columns,
        name="columns",
        out_shape=jax.ShapeDtypeStruct((2, 8, 512, 256), BF16),
        in_specs=[hbm, hbm],
        out_specs=hbm,
        scratch_shapes=[
            pltpu.VMEM((2, 512, 512), BF16),
            pltpu.VMEM((2, 512, 2048), BF16),
            pltpu.VMEM((2, 8, 512, 256), BF16),
            dma, dma((8,)), dma((2, 8)),
        ],
        compiler_params=pltpu.CompilerParams(vmem_limit_bytes=60 << 20),
        cost_estimate=pl.CostEstimate(flops=4 << 30, bytes_accessed=10 << 20, transcendentals=0),
    )(jnp.asarray(column_table()), rows.reshape(2, 512, 2048))


def solution(mesh):
    placed = (P("chan", "tile", None), P(), P("tile"), P())
    return jax.shard_map(
        shards, mesh=mesh, in_specs=placed, out_specs=P(None, "chan", None, "tile"), check_vma=False
    )
```

time: 149 us -> 138 us (0.926)
  the two profiles are of different devices: /device:TPU:47 before, /device:TPU:1 now
where the time goes in v2:
time: 138 us
  Pallas kernels  138 us (100%)
    pallas_call x1, Pallas kernels, shards(): pl.pallas_call(mix_rows, name='mix_rows', out_shape=jax.ShapeDtypeStruct(...  132 us
    pallas_call x1, Pallas kernels, shards(): pl.pallas_call(columns, name='columns', out_shape=jax.ShapeDtypeStruct((2...  5.59 us

profile of v2, /device:TPU:1, one launch (start us, length us, event | category | flops | bytes accessed | tf_op | source)
XLA Modules:
  0.0 137.8 jit_solution(5713757199747915222)
XLA Ops:
  0.0 132.0 %mix_rows.1 = bf16[2,2,256,2048]{3,2,1,0:T(8,128)(2,1)} custom-call(f32[1024,1024]{1,0:T(8,128)} %bitcast.4, f32[512,512]{1,0:T(8,128)} %op.1, f32[1,128]{1,0:T(1,128)} %bitcast.6, f32[1,1024]{1,0:T(1,128)} %bitcast.5, bf16[4,1024,512]{2,1,0:T(8,128)(2,1)} %constant.4.clone.ytab), custom_call_target="tpu_custom_call" | custom-call | flops 8589934592 | bytes 16777216 | tf_op jit(solution)/shard_map/mix_rows/pallas_call | solution.py:327
  132.0 5.6 %columns.1 = bf16[2,8,512,256]{3,2,1,0:T(8,128)(2,1)} custom-call(bf16[2,512,512]{2,1,0:T(8,128)(2,1)} %constant.5.clone.table, bf16[2,512,2048]{2,1,0:T(8,128)(2,1)} %bitcast.7), custom_call_target="tpu_custom_call" | custom-call | flops 4294967296 | bytes 10485760 | tf_op jit(solution)/shard_map/columns/pallas_call | solution.py:351

commit v3 on v2

--- a/solution.py
+++ b/solution.py
@@ -17,7 +17,7 @@
 PEERS = 63 + 32 + 2
 LAG = 5
 EARLY = 8
-GROUP = 4
+GROUP = 2
 
 
 def tables(count):
@@ -44,9 +44,9 @@
     return np.stack(halves).astype(ml_dtypes.bfloat16)
 
 
-def mix_rows(cube, op, taper_x, taper_y, ytab, rows_out,
-             op_here, held, sent, mixed_in, op2, tapered, land, table, wide, rows,
-             cube_sem, table_sem, op_sem, out_sem, send1, recv1, send2, land_sem,
+def mix_rows(cube, op, taper_x, taper_y, ytab, xtab, rows, xtab_here,
+             tx_here, ty_here, op_here, held, sent, mixed_in, op2, tapered, land, table, wide,
+             cube_sem, table_sem, op_sem, xtab_sem, taper_sem, send1, recv1, send2, land_sem,
              send_fwd, fwd_sem, send_sib, sib_sem, sibf_sem):
     c = lax.axis_index("chan")
     t = lax.axis_index("tile")
@@ -110,6 +110,12 @@
     table_load.start()
     op_load = pltpu.make_async_copy(op, op_here, op_sem)
     op_load.start()
+    xtab_load = pltpu.make_async_copy(xtab, xtab_here, xtab_sem)
+    xtab_load.start()
+    taper_loads = [pltpu.make_async_copy(taper_x, tx_here, taper_sem.at[0]),
+                   pltpu.make_async_copy(taper_y, ty_here, taper_sem.at[1])]
+    for load in taper_loads:
+        load.start()
 
     c2 = lax.broadcasted_iota(jnp.int32, (512, 1024), 0)
     spread_k = jnp.where(lax.broadcasted_iota(jnp.int32, (512, 1024), 1) // 2 == c2, 1.0, 0.0).astype(BF16)
@@ -128,7 +134,9 @@
 
     lax.fori_loop(0, 4, expand, 0)
     odd = lax.broadcasted_iota(jnp.int32, (256, 256), 0) % 2 == 1
-    tx = jnp.where(odd, taper_x[0, c + 64], taper_x[0, c])
+    for load in taper_loads:
+        load.wait()
+    tx = jnp.where(odd, tx_here[0, c + 64], tx_here[0, c])
     table_load.wait()
 
     def mix(st, half):
@@ -138,7 +146,7 @@
         for n in range(2):
             cols = slice(512 * half + 256 * n, 512 * half + 256 * n + 256)
             part = jnp.dot(op2[pl.ds(start, 256), :], mixed_in[:, cols], preferred_element_type=F32)
-            tapered[pl.ds(start, 256), cols] = (part * tx * taper_y[:, cols]).astype(BF16)
+            tapered[pl.ds(start, 256), cols] = (part * tx * ty_here[:, cols]).astype(BF16)
         return zh, start
 
     here = pl.ds(pl.multiple_of(x * 64 + y * 16, 16), 16)
@@ -231,14 +239,13 @@
             part = jnp.dot(land[g], table[:, 256 * n:256 * n + 256], preferred_element_type=F32)
             wide[2 * n] = part[:, :128]
             wide[2 * n + 1] = part[:, 128:]
-        span = pl.ds(pl.multiple_of(g * 16, 16), 16)
+        spans = [pl.ds(pl.multiple_of(256 * part + g * 16, 16), 16) for part in range(2)]
         for ch in range(8):
             for par in range(2):
                 for n in range(4):
                     two = [wide[n, pl.ds(2 * ch + r + 16 * par, 8, stride=32), :] for r in range(2)]
                     at = 256 * ch + 128 * (n % 2)
-                    rows[par, n // 2, span, at:at + 128] = jnp.concatenate(two).astype(BF16)
-        pltpu.make_async_copy(rows.at[:, :, span], rows_out.at[:, :, span], out_sem).start()
+                    rows[par, spans[n // 2], at:at + 128] = jnp.concatenate(two).astype(BF16)
 
     mix_half(0)
 
@@ -285,7 +292,7 @@
                 take_sibling(st, passed, sibf_sem if passed else sib_sem)
             transform(group_of(st, passed, other_core))
 
-    pltpu.make_async_copy(rows, rows_out, out_sem).wait()
+    xtab_load.wait()
     less = pl.ds(0, 63 * 16)
     pltpu.make_async_copy(sent.at[less], mixed_in.at[less], send1).wait()
     pltpu.make_async_copy(tapered.at[less], tapered.at[less], send2).wait()
@@ -293,22 +300,15 @@
     pltpu.make_async_copy(land.at[pl.ds(0, 8)], land.at[pl.ds(0, 8)], send_sib).wait()
 
 
-def columns(table, rows, out, table_here, rows_here, out_here, table_sem, rows_sem, out_sem):
-    width = 256 * GROUP
-    cols = [slice(width * q, width * q + width) for q in range(8 // GROUP)]
-    loads = [pltpu.make_async_copy(table, table_here, table_sem)]
-    loads += [pltpu.make_async_copy(rows.at[:, :, some], rows_here.at[:, :, some], rows_sem.at[q]) for q, some in enumerate(cols)]
-    for load in loads:
-        load.start()
-    loads[0].wait()
+def columns(table, rows, out, out_here, out_sem):
     stores = []
-    for q, some in enumerate(cols):
-        loads[1 + q].wait()
+    for q in range(8 // GROUP):
+        some = slice(256 * GROUP * q, 256 * GROUP * (q + 1))
         chans = slice(GROUP * q, GROUP * q + GROUP)
         for part in range(2):
             span = slice(256 * part, 256 * part + 256)
-            even = jnp.dot(table_here[0, span], rows_here[0, :, some], preferred_element_type=F32)
-            odd = jnp.dot(table_here[1, span], rows_here[1, :, some], preferred_element_type=F32)
+            even = jnp.dot(table[0, span], rows[0, :, some], preferred_element_type=F32)
+            odd = jnp.dot(table[1, span], rows[1, :, some], preferred_element_type=F32)
             plus, minus = (even + odd).astype(BF16), (even - odd).astype(BF16)
             for n in range(GROUP):
                 out_here[part, GROUP * q + n, :256] = plus[:, 256 * n:256 * n + 256]
@@ -324,13 +324,22 @@
     vmem = pl.BlockSpec(memory_space=pltpu.VMEM)
     hbm = pl.BlockSpec(memory_space=pl.ANY)
     dma = pltpu.SemaphoreType.DMA
-    rows = pl.pallas_call(
+
+    def in_hbm(array):
+        return pltpu.with_memory_space_constraint(array, pltpu.HBM)
+
+    def in_vmem(array):
+        return pltpu.with_memory_space_constraint(array, pltpu.VMEM)
+
+    rows, xtab = pl.pallas_call(
         mix_rows,
         name="mix_rows",
-        out_shape=jax.ShapeDtypeStruct((2, 2, 256, 2048), BF16),
-        in_specs=[hbm, hbm, pl.BlockSpec(memory_space=pltpu.SMEM), vmem, hbm],
-        out_specs=hbm,
+        out_shape=[pltpu.VMEM((2, 512, 2048), BF16), pltpu.VMEM((2, 512, 512), BF16)],
+        in_specs=[hbm] * 6,
+        out_specs=[vmem, vmem],
         scratch_shapes=[
+            pltpu.SMEM((1, 128), F32),
+            pltpu.VMEM((1, 1024), F32),
             pltpu.VMEM((512, 512), F32),
             pltpu.VMEM((8, 1024, 128), F32),
             pltpu.VMEM((1024, 1024), BF16),
@@ -340,29 +349,24 @@
             pltpu.VMEM((16, 256, 1024), BF16),
             pltpu.VMEM((1024, 512), BF16),
             pltpu.VMEM((4, 256, 128), F32),
-            pltpu.VMEM((2, 2, 256, 2048), BF16),
-            dma((8,)), dma, dma, dma, dma, dma((2,)), dma, dma((32,)),
+            dma((8,)), dma, dma, dma, dma((2,)), dma, dma((2,)), dma, dma((32,)),
             dma, dma((32,)), dma, dma((16,)), dma((16,)),
         ],
         compiler_params=pltpu.CompilerParams(
-            collective_id=0, has_side_effects=True, vmem_limit_bytes=56 << 20),
+            collective_id=0, has_side_effects=True, vmem_limit_bytes=38 << 20),
         cost_estimate=pl.CostEstimate(flops=8 << 30, bytes_accessed=16 << 20, transcendentals=0),
-    )(cube.reshape(1024, 1024), residual_op, taper_x.reshape(1, 128), taper_y.reshape(1, 1024), jnp.asarray(row_tables()))
+    )(in_hbm(cube.reshape(1024, 1024)), in_hbm(residual_op), in_hbm(taper_x.reshape(1, 128)),
+      in_hbm(taper_y.reshape(1, 1024)), in_hbm(jnp.asarray(row_tables())), in_hbm(jnp.asarray(column_table())))
     return pl.pallas_call(
         columns,
         name="columns",
         out_shape=jax.ShapeDtypeStruct((2, 8, 512, 256), BF16),
-        in_specs=[hbm, hbm],
+        in_specs=[vmem, vmem],
         out_specs=hbm,
-        scratch_shapes=[
-            pltpu.VMEM((2, 512, 512), BF16),
-            pltpu.VMEM((2, 512, 2048), BF16),
-            pltpu.VMEM((2, 8, 512, 256), BF16),
-            dma, dma((8,)), dma((2, 8)),
-        ],
-        compiler_params=pltpu.CompilerParams(vmem_limit_bytes=60 << 20),
+        scratch_shapes=[pltpu.VMEM((2, 8, 512, 256), BF16), dma((2, 8))],
+        compiler_params=pltpu.CompilerParams(vmem_limit_bytes=24 << 20),
         cost_estimate=pl.CostEstimate(flops=4 << 30, bytes_accessed=10 << 20, transcendentals=0),
-    )(jnp.asarray(column_table()), rows.reshape(2, 512, 2048))
+    )(in_vmem(xtab), in_vmem(rows))
 
 
 def solution(mesh):

time: 138 us -> 134 us (0.971)
  Pallas kernels: 138 us -> 134 us
    pallas_call x1, Pallas kernels: 5.59 us -> 3.33 us  [shards(): pl.pallas_call(columns, name='columns', out_shape=jax.ShapeDtypeStruct((2...]
    pallas_call x1, Pallas kernels: 132 us -> 131 us  [shards(): pl.pallas_call(mix_rows, name='mix_rows', out_shape=[pltpu.VMEM((2, 512,...]
where the time goes in v3:
time: 134 us
  Pallas kernels  134 us (100%)
    pallas_call x1, Pallas kernels, shards(): pl.pallas_call(mix_rows, name='mix_rows', out_shape=[pltpu.VMEM((2, 512,...  131 us
    pallas_call x1, Pallas kernels, shards(): pl.pallas_call(columns, name='columns', out_shape=jax.ShapeDtypeStruct((2...  3.33 us

profile of v3, /device:TPU:1, one launch (start us, length us, event | category | flops | bytes accessed | tf_op | source)
XLA Modules:
  0.0 134.1 jit_solution(3808219480061760006)
XLA Ops:
  0.0 130.6 %mix_rows.1 = (bf16[2,512,2048]{2,1,0:T(8,128)(2,1)S(1)}, bf16[2,512,512]{2,1,0:T(8,128)(2,1)S(1)}) custom-call(f32[1024,1024]{1,0:T(8,128)} %bitcast.3, f32[512,512]{1,0:T(8,128)} %op.1, f32[1,128]{1,0:T(1,128)} %bitcast.5, f32[1,1024]{1,0:T(1,128)} %bitcast.4, bf16[4,1024,512]{2,1,0:T(8,128)(2,1)} %constant.4.clone.ytab, ...), custom_call_target="tpu_custom_call" | custom-call | flops 8589934592 | bytes 16777216 | tf_op jit(solution)/shard_map/mix_rows/pallas_call | solution.py:334
  130.6 3.3 %columns.1 = bf16[2,8,512,256]{3,2,1,0:T(8,128)(2,1)} custom-call(bf16[2,512,512]{2,1,0:T(8,128)(2,1)S(1)} %get-tuple-element.7.table, bf16[2,512,2048]{2,1,0:T(8,128)(2,1)S(1)} %get-tuple-element.8.rows), custom_call_target="tpu_custom_call" | custom-call | flops 4294967296 | bytes 10485760 | tf_op jit(solution)/shard_map/columns/pallas_call | solution.py:360

commit v4 on v3

--- a/solution.py
+++ b/solution.py
@@ -17,7 +17,7 @@
 PEERS = 63 + 32 + 2
 LAG = 5
 EARLY = 8
-GROUP = 2
+GROUP = 1
 
 
 def tables(count):
@@ -57,7 +57,7 @@
     sibling = (c, zl * 2 + 1 - co)
 
     loads = [pltpu.make_async_copy(cube.at[:, pl.ds(128 * k, 128)], held.at[k], cube_sem.at[k]) for k in range(8)]
-    for load in loads:
+    for load in loads[:4]:
         load.start()
     barrier = pltpu.get_barrier_semaphore()
 
@@ -79,6 +79,8 @@
     for other in (partner, sibling):
         pl.semaphore_signal(barrier, inc=1, device_id=other, device_id_type=MESH)
 
+    for load in loads[4:]:
+        load.start()
     halves = (slice(0, 512), slice(512, 1024))
     mine = pl.ds(pl.multiple_of(c * 16, 16), 16)
 
@@ -102,7 +104,7 @@
                 device_id=(d, t), device_id_type=MESH).start()
             return 0
 
-        lax.fori_loop(1, 64, scatter, 0)
+        lax.fori_loop(1, 64, scatter, 0, unroll=3)
         own1 = pltpu.make_async_copy(cast(c, half), to, recv1.at[half])
         own1.start()
 
@@ -140,7 +142,7 @@
     table_load.wait()
 
     def mix(st, half):
-        delta = jnp.where(st == 0, 0, jnp.where(st == 1, -u, jnp.where(st == 2, u, 2)))
+        delta = (0, -u, u, 2)[st]
         zh = (j + delta + 4) % 4
         start = pl.multiple_of(zh * 256, 256)
         for n in range(2):
@@ -151,45 +153,47 @@
 
     here = pl.ds(pl.multiple_of(x * 64 + y * 16, 16), 16)
 
-    def send_rows(st, half, k, zh, start):
-        to_tile = jnp.where(st % 2 == 1, across, t)
-        dx = (x + k // 4) % 4
-        dy = (y + k % 4) % 4
+    slot = t * 4 + j
+    dys = [(y + f) % 4 for f in range(4)]
+
+    def send_rows(st, half, e, dx, dy, zh, start):
+        to_tile = across if st % 2 == 1 else t
         pltpu.make_async_remote_copy(
             src_ref=tapered.at[pl.ds(pl.multiple_of(start + dx * 64 + dy * 16, 16), 16), halves[half]],
-            dst_ref=land.at[t * 4 + j, here, halves[half]], send_sem=send2,
-            recv_sem=land_sem.at[half * 16 + st * 4 + k // 4],
+            dst_ref=land.at[slot, here, halves[half]], send_sem=send2, recv_sem=land_sem.at[half * 16 + st * 4 + e],
             device_id=(dx * 16 + zh * 4 + dy, to_tile), device_id_type=MESH).start()
 
     def mix_half(half):
         pltpu.make_async_copy(sent.at[:, halves[half]], mixed_in.at[:, halves[half]], recv1.at[half]).wait()
         zh2, start2 = mix(2, half)
         zh0, start0 = mix(0, half)
-        send_rows(2, half, 0, zh2, start2)
+        send_rows(2, half, 0, x, y, zh2, start2)
         own2 = pltpu.make_async_copy(
             tapered.at[pl.ds(pl.multiple_of(start0 + x * 64 + y * 16, 16), 16), halves[half]],
-            land.at[t * 4 + j, here, halves[half]], land_sem.at[half * 16])
+            land.at[slot, here, halves[half]], land_sem.at[half * 16])
         own2.start()
-
-        def both(k, _):
-            send_rows(2, half, k, zh2, start2)
-            send_rows(0, half, k, zh0, start0)
+        for dy in dys[1:]:
+            send_rows(2, half, 0, x, dy, zh2, start2)
+            send_rows(0, half, 0, x, dy, zh0, start0)
+
+        def both(e, _):
+            dx = (x + e) % 4
+            for dy in dys:
+                send_rows(2, half, e, dx, dy, zh2, start2)
+                send_rows(0, half, e, dx, dy, zh0, start0)
             return 0
 
-        lax.fori_loop(1, 16, both, 0)
-
-        def alone(n, _):
-            st = 2 * n + 1
+        lax.fori_loop(1, 4, both, 0)
+        for st in (1, 3):
             zh, start = mix(st, half)
 
-            def one(k, _):
-                send_rows(st, half, k, zh, start)
+            def one(e, _, st=st, zh=zh, start=start):
+                dx = (x + e) % 4
+                for dy in dys:
+                    send_rows(st, half, e, dx, dy, zh, start)
                 return 0
 
-            lax.fori_loop(0, 16, one, 0)
-            return 0
-
-        lax.fori_loop(0, 2, alone, 0)
+            lax.fori_loop(0, 4, one, 0)
 
     def group_of(st, passed, other_core):
         z = zl + passed - 2 * zl * passed

time: 134 us -> 134 us (level)
  no operation moved by 1% of the time
where the time goes in v4:
time: 134 us
  Pallas kernels  134 us (100%)
    pallas_call x1, Pallas kernels, shards(): pl.pallas_call(mix_rows, name='mix_rows', out_shape=[pltpu.VMEM((2, 512,...  131 us
    pallas_call x1, Pallas kernels, shards(): pl.pallas_call(columns, name='columns', out_shape=jax.ShapeDtypeStruct((2...  3.22 us

profile of v4, /device:TPU:1, one launch (start us, length us, event | category | flops | bytes accessed | tf_op | source)
XLA Modules:
  0.0 134.0 jit_solution(11545322480513157981)
XLA Ops:
  0.0 130.6 %mix_rows.1 = (bf16[2,512,2048]{2,1,0:T(8,128)(2,1)S(1)}, bf16[2,512,512]{2,1,0:T(8,128)(2,1)S(1)}) custom-call(f32[1024,1024]{1,0:T(8,128)} %bitcast.3, f32[512,512]{1,0:T(8,128)} %op.1, f32[1,128]{1,0:T(1,128)} %bitcast.5, f32[1,1024]{1,0:T(1,128)} %bitcast.4, bf16[4,1024,512]{2,1,0:T(8,128)(2,1)} %constant.4.clone.ytab, ...), custom_call_target="tpu_custom_call" | custom-call | flops 8589934592 | bytes 16777216 | tf_op jit(solution)/shard_map/mix_rows/pallas_call | solution.py:338
  130.6 3.2 %columns.1 = bf16[2,8,512,256]{3,2,1,0:T(8,128)(2,1)} custom-call(bf16[2,512,512]{2,1,0:T(8,128)(2,1)S(1)} %get-tuple-element.7.table, bf16[2,512,2048]{2,1,0:T(8,128)(2,1)S(1)} %get-tuple-element.8.rows), custom_call_target="tpu_custom_call" | custom-call | flops 4294967296 | bytes 10485760 | tf_op jit(solution)/shard_map/columns/pallas_call | solution.py:364
